TPU v7x, 256 devices: a whole 4x4x8 slice. The times are simulated.
256 devices in a mesh: dp: 32 (over x, z), tensor: 8 (over y, core).
Axes of the slice: x: 4, y: 4, z: 8, core: 2. Of those that a mesh axis runs over, the one named last changes fastest.
Arguments:
- momentum: float32 [32, 8192, 1024], P('dp', None, 'tensor'), may hold values from -6 to 6
- gradient: bfloat16 [32, 8192, 1024], P('dp', None, 'tensor'), may hold values from -6 to 6
- masters: float32 [8192, 1024], P('dp', 'tensor'), may hold values from -6 to 6
- tokens: bfloat16 [4096, 8192], P('dp', 'tensor'), may hold values from -6 to 6
- freq_index: int32 [8, 1024], P('tensor'), may hold values from 0 to 8191, as said below
Outputs:
- residual: float32 [32, 8192, 1024], P('dp', None, 'tensor')
- new_masters: float32 [8192, 1024], P('dp', 'tensor')
- keys_out: bfloat16 [4096, 1024], P('dp', 'tensor')
Inputs may be any that keep to these rules, and one draw needn't show every extreme that they name: `freq_index`: each row lists 1024 distinct frequencies, 0 and 8191 among them; the same list serves every replica.
All inputs are finite; a program needn't handle non-finite values.
Results may differ from a plain program's by a relative error of at most 0.007.
Values may be sent and summed in bfloat16 or wider, within the bound.
A program may use at most 64 MiB of HBM per device.

v0:
```python
import math

import jax
import jax.numpy as jnp
from jax import lax
from jax.sharding import PartitionSpec as P

momentum_decay = 0.9
step_rate = 1.0


def cosine_rows(frequency, row_count, model_width):
    positions = lax.iota(jnp.int32, row_count)
    phases = (2 * positions + 1)[None, :] * frequency[:, None] % (4 * model_width)
    angles = phases.astype(jnp.float32) * (math.pi / (2 * model_width))
    scales = jnp.where(
        frequency == 0, math.sqrt(1.0 / model_width), math.sqrt(2.0 / model_width)
    ).astype(jnp.float32)
    return (scales[:, None] * jnp.cos(angles)).astype(jnp.bfloat16)


def body(momentum, gradient, masters, tokens, freq_index):
    replica_count = lax.axis_size("dp")
    own_rows = masters.shape[0]
    model_width = momentum.shape[1]
    freq_count = freq_index.shape[1]
    piece_rows = min(512, freq_count)
    gathered = lax.all_gather(tokens, "tensor", axis=1, tiled=True)
    states = momentum_decay * momentum[0] + gradient[0].astype(jnp.float32)
    states_low = states.astype(jnp.bfloat16)
    remain = states
    pieces = []
    for freq_piece in range(freq_count // piece_rows):
        lower = freq_piece * piece_rows
        cosines = cosine_rows(freq_index[0, lower : lower + piece_rows], model_width, model_width)
        coefficient = jnp.dot(cosines, states_low, preferred_element_type=jnp.float32).astype(
            jnp.bfloat16
        )
        remain = remain - jnp.dot(cosines.T, coefficient, preferred_element_type=jnp.float32)
        pieces.append(coefficient)
    own_coeffs = [jnp.concatenate(pieces, axis=0)]
    residual = remain[None]
    stacked = jnp.stack(own_coeffs)
    update = (
        lax.psum_scatter(
            jnp.dot(
                cosine_rows(freq_index[0], own_rows * lax.axis_size("dp"), model_width).T,
                stacked[0],
                preferred_element_type=jnp.float32,
            ).astype(jnp.bfloat16),
            "dp",
            scatter_dimension=0,
            tiled=True,
        ).astype(jnp.float32)
        / replica_count
    )
    new_masters = masters - step_rate * update
    weights = new_masters.astype(jnp.bfloat16)
    products = jnp.dot(
        gathered,
        lax.all_gather(weights, "dp", axis=0, tiled=True),
        preferred_element_type=jnp.float32,
    )
    projected = (products * model_width ** (-0.5)).astype(jnp.bfloat16)
    return (residual, new_masters, projected)


def solution(mesh):
    return jax.shard_map(
        body,
        mesh=mesh,
        in_specs=(
            P("dp", None, "tensor"),
            P("dp", None, "tensor"),
            P("dp", "tensor"),
            P("dp", "tensor"),
            P("tensor", None),
        ),
        out_specs=(P("dp", None, "tensor"), P("dp", "tensor"), P("dp", "tensor")),
        check_vma=False,
    )
```

profile of v0, /device:TPU:8, one launch (start us, length us, event | category | flops | bytes accessed | tf_op | source)
XLA Modules:
  0.0 627.0 jit_solution(13688933179937345676)
XLA Ops:
  8.0 0.0 reduce-scatter.2.cloned.1.call-start
  8.1 0.0 copy-start
  8.1 0.0 copy-start.1
  8.1 3.5 bitcast_convert_fusion.9
  11.6 0.5 copy-done
  12.1 0.7 copy-done.1
  12.8 0.7 bitcast_convert_fusion.10
  13.5 0.0 copy-done.3
  13.5 62.5 %fusion.25 = bf16[512,128]{1,0:T(8,128)(2,1)S(1)} fusion(s32[512]{0:T(512)S(1)} %bitcast.34, f32[512]{0:T(512)S(1)} %compare_select_fusion.1, s32[8192]{0:T(1024)S(1)} %multiply_add_fusion, bf16[8192,128]{1,0:T(8,128)(2,1)S(1)} %bitcast_convert_fusion.9), kind=kOutput, calls=%fused_computation.38 | convolution fusion | flops 1140850688 | bytes 2265088 | tf_op jit(solution)/shard_map/dot_general | solution.py:36
  76.0 62.6 %fusion.28 = bf16[512,128]{1,0:T(8,128)(2,1)S(1)} fusion(s32[512]{0:T(512)S(1)} %bitcast.37, s32[8192]{0:T(1024)S(1)} %multiply_add_fusion, f32[512]{0:T(512)S(1)} %compare_select_fusion.2, bf16[8192,128]{1,0:T(8,128)(2,1)S(1)} %bitcast_convert_fusion.10), kind=kOutput, calls=%fused_computation.39 | convolution fusion | flops 1140850688 | bytes 2265088 | tf_op jit(solution)/shard_map/dot_general | solution.py:36
  138.6 0.0 copy-start.2
  138.6 127.9 %fusion.21 = bf16[8192,128]{1,0:T(8,128)(2,1)} fusion(s32[1024]{0:T(1024)S(1)} %bitcast.32, s32[8192]{0:T(1024)S(1)} %multiply_add_fusion, f32[1024]{0:T(1024)S(1)} %compare_select_fusion, bf16[1024,128]{1,0:T(8,128)(2,1)S(1)} %fusion.82), kind=kOutput, calls=%fused_computation.37 | convolution fusion | flops 2282749952 | bytes 2400256 | tf_op jit(solution)/shard_map/dot_general | solution.py:46
  266.5 0.0 reduce-scatter.2.cloned.1.call-update
  266.5 0.0 all-gather.5.cloned.1.call-start
  266.6 0.5 all-gather.5.cloned.1.call-update
  267.1 0.0 all-gather.3.cloned.1.call-start
  267.2 218.8 %reduce-scatter.2.cloned.1.call-done = bf16[256,128]{1,0:T(8,128)(2,1)} async-done(((bf16[8192,128]{1,0:T(8,128)(2,1)}), bf16[256,128]{1,0:T(8,128)(2,1)}) %reduce-scatter.2.cloned.1.call-update) | async-done | bytes 65552 | tf_op jit(solution)/shard_map/reduce_scatter | solution.py:45
  485.9 0.0 copy-done.2
  485.9 1.5 fusion.58
  487.5 0.0 all-gather.3.cloned.1.call-update
  487.5 64.4 %convolution_subtract_fusion.1 = f32[8192,128]{1,0:T(8,128)S(1)} fusion(s32[512]{0:T(512)S(1)} %bitcast.38, s32[8192]{0:T(1024)S(1)} %multiply_add_fusion, f32[512]{0:T(512)S(1)} %compare_select_fusion.2, bf16[512,128]{1,0:T(8,128)(2,1)S(1)} %fusion.28, bf16[1,8192,128]{2,1,0:T(8,128)(2,1)S(1)} %copy-done.1, f32[1,8192,128]{2,1,0:T(8,128)} %param.5), kind=kOutput, calls=%fused_computation.36 | convolution fusion | flops 1145044992 | bytes 10653696 | tf_op jit(solution)/shard_map/dot_general | solution.py:39
  551.9 63.7 %fusion.20 = f32[1,8192,128]{2,1,0:T(8,128)} fusion(f32[8192,128]{1,0:T(8,128)S(1)} %convolution_subtract_fusion.1, s32[512]{0:T(512)S(1)} %bitcast.35, f32[512]{0:T(512)S(1)} %compare_select_fusion.1, s32[8192]{0:T(1024)S(1)} %multiply_add_fusion, bf16[512,128]{1,0:T(8,128)(2,1)S(1)} %fusion.25), kind=kOutput, calls=%fused_computation.35 | convolution fusion | flops 1141899264 | bytes 8556544 | tf_op jit(solution)/shard_map/dot_general | solution.py:39
  615.5 3.0 fusion.33
  618.5 0.7 copy.8
  (9 shorter events, 0.0 us)
Async XLA Ops:
  8.0 477.9 %reduce-scatter.2.cloned.1.call-start = ((), (), s32[]{:S(2)}) async-start(), calls=%async_computation.1 | async-start | bytes 2162688 | tf_op jit(solution)/shard_map/reduce_scatter | solution.py:45
  8.1 4.0 copy-start
  8.1 4.7 copy-start.1
  12.8 0.7 copy-start.3
  138.6 347.3 %copy-start.2 = (f32[256,128]{1,0:T(8,128)S(1)}, f32[256,128]{1,0:T(8,128)}, u32[]{:S(2)}) copy-start(f32[256,128]{1,0:T(8,128)} %param.7) | copy-start | bytes 393220
  266.5 349.0 %all-gather.5.cloned.1.call-start = ((), (), s32[]{:S(2)}) async-start(), calls=%async_computation.3 | async-start | bytes 2359296 | tf_op jit(solution)/shard_map/all_gather | solution.py:28
  267.1 348.4 %all-gather.3.cloned.1.call-start = ((), (), s32[]{:S(2)}) async-start(), calls=%async_computation.2 | async-start | bytes 2162688 | tf_op jit(solution)/shard_map/all_gather | solution.py:61
Sparse Core Ops, SparseCore 0:
  266.6 219.2 reduce-scatter.1
Sparse Core Ops, SparseCore 1:
  269.0 29.6 all-gather.4
  487.6 76.5 all-gather.2
where the time goes:
time: 639 us; the launch traced here: 627 us
  matrix products  384 us (60%)
  waiting for transfers between devices  219 us (34%)
  between operations  16 us (3%)
    reduce_scatter x1, waiting for transfers between devices, body(): lax.psum_scatter(jnp.dot(cosine_rows(freq_index[0], own_rows * lax.axis_s...  219 us
    dot_general x2, matrix products, body(): jnp.dot(cosines.T, coefficient, preferred_element_type=jnp.float32)  128 us
    dot_general x1, matrix products, body(): jnp.dot(cosine_rows(freq_index[0], own_rows * lax.axis_size('dp'), model_...  128 us
    dot_general x2, matrix products, body(): jnp.dot(cosines, states_low, preferred_element_type=jnp.float32)  125 us
  transfers between devices with their start and end apart: 3, of which 1 were waited for; matrix products, arithmetic and copies ran while one was open for 21% of the time, Pallas kernels for 0%

commit v1 on v0

v1 whole, which is shorter than its diff:
```python
import math

import jax
import jax.numpy as jnp
from jax import lax
from jax.experimental import pallas as pl
from jax.experimental.pallas import tpu as pltpu
from jax.sharding import PartitionSpec as P

D = 8192
H = D // 2
K = 1024
CB = 128
X, Z = 4, 8
REPLICAS = X * Z
R = 256
T = 128
RA = 160
RB = R - RA
BF = jnp.bfloat16
F32 = jnp.float32

TOK, AR, AL, AX, BX, BR, BL, CX, CZ, GZ, GX, MSGS = 0, 8, 12, 15, 19, 23, 26, 30, 33, 40, 47, 50


def dot(a, b):
    return jnp.dot(a, b, preferred_element_type=F32)


def dot_nt(a, b):
    return lax.dot_general(a, b, (((1,), (1,)), ((), ())), preferred_element_type=F32)


def cos_sin(phase):
    quadrant = (phase + 4096) >> 13
    angle = (phase - (quadrant << 13)).astype(F32) * (math.pi / 16384)
    square = angle * angle
    sine = angle * (1.0 + square * (-1 / 6 + square * (1 / 120 + square * (-1 / 5040))))
    cosine = 1.0 + square * (-0.5 + square * (1 / 24 + square * (-1 / 720 + square * (1 / 40320))))
    swap = (quadrant & 1) == 1
    c = jnp.where(swap, sine, cosine)
    s = jnp.where(swap, cosine, sine)
    c = jnp.where(((quadrant + 1) & 2) == 2, -c, c)
    s = jnp.where((quadrant & 2) == 2, -s, s)
    return c, s


def kernel(mom, grad, mast, tok_in, freq, res, newm, keys,
           state, gbuf, table, xt, seo, coef, rsx, rszs, rszr, sbuf, tok, tt, left, wbuf, mbuf, fbuf,
           ca, sa, ldsem, stsem, ssem, rsem):
    i = lax.axis_index("dp")
    t = lax.axis_index("tensor")
    x, z = i // Z, i % Z
    y, core = t // 2, t % 2

    def xdev(d):
        return (((x + d) % X) * Z + z, t)

    def zdev(d):
        return (x * Z + (z + d) % Z, t)

    def ydev(d):
        return (i, ((y + d) % 4) * 2 + core)

    twin = (i, y * 2 + (1 - core))

    barrier = pltpu.get_barrier_semaphore()
    peers = [xdev(d) for d in range(1, X)] + [zdev(d) for d in range(1, Z)] + [ydev(1), ydev(3), twin]
    for peer in peers:
        pl.semaphore_signal(barrier, inc=1, device_id=peer, device_id_type=pl.DeviceIdType.MESH)

    load_mast = pltpu.make_async_copy(mast, mbuf, ldsem.at[0])
    load_freq = pltpu.make_async_copy(freq, fbuf, ldsem.at[1])
    load_tok = pltpu.make_async_copy(tok_in, tok.at[t], ldsem.at[2])
    load_mast.start()
    load_freq.start()
    load_tok.start()
    loads = []
    for c in (0, 7, 1, 6, 2, 5, 3, 4):
        rows = pl.ds(1024 * c, 1024)
        a = pltpu.make_async_copy(mom.at[0, rows], state.at[rows], ldsem.at[3 + c])
        b = pltpu.make_async_copy(grad.at[0, rows], gbuf.at[rows], ldsem.at[11 + c])
        a.start()
        b.start()
        loads.append((a, b))

    sent = []

    def send(number, src, dst, device):
        copy = pltpu.make_async_remote_copy(
            src_ref=src, dst_ref=dst, send_sem=ssem.at[number], recv_sem=rsem.at[number],
            device_id=device, device_id_type=pl.DeviceIdType.MESH)
        copy.start()
        sent.append(copy)

    def arrived(number, ref):
        pltpu.make_async_remote_copy(
            src_ref=ref, dst_ref=ref, send_sem=ssem.at[number], recv_sem=rsem.at[number],
            device_id=twin, device_id_type=pl.DeviceIdType.MESH).wait_recv()

    load_mast.wait()
    wbuf[x, z] = mbuf[...].astype(BF)
    load_tok.wait()
    pl.semaphore_wait(barrier, len(peers))

    def a_block(xx, zz):
        return wbuf.at[xx % X, zz % Z, pl.ds(0, RA)]

    def a_right(s):
        send(AR + s, a_block(x, z - s + Z), a_block(x, z - s + Z), zdev(1))

    def a_left(s):
        send(AL + s, a_block(x, z + s), a_block(x, z + s), zdev(-1 + Z))

    def a_right_in(s):
        arrived(AR + s, a_block(x, z - 1 - s + Z))

    def a_left_in(s):
        arrived(AL + s, a_block(x, z + 1 + s))

    def a_plane(xx, lo, n):
        return wbuf.at[xx % X, pl.ds(lo, n), pl.ds(0, RA)]

    def b_part(xx, lo, n):
        return wbuf.at[xx % X, z, pl.ds(RA + lo, n)]

    def b_plane(zz):
        return wbuf.at[:, zz % Z, pl.ds(RA, RB)]

    def b_right(s):
        send(BR + s, b_plane(z - s + Z), b_plane(z - s + Z), zdev(1))

    def b_left(s):
        send(BL + s, b_plane(z + s), b_plane(z + s), zdev(-1 + Z))

    def b_right_in(s):
        arrived(BR + s, b_plane(z - 1 - s + Z))

    def b_left_in(s):
        arrived(BL + s, b_plane(z + 1 + s))

    def tok_half(yy, lo, n):
        return tok.at[(yy % 4) * 2 + core, pl.ds(lo, n)]

    def tok_twin(yy):
        return tok.at[(yy % 4) * 2 + 1 - core]

    send(TOK + 0, tok_half(y, 0, T), tok_half(y, 0, T), ydev(1))
    send(TOK + 1, tok_half(y, 0, T), tok_half(y, 0, T), ydev(3))
    a_right(0)
    a_left(0)
    send(BX + 0, b_part(x, 0, RB), b_part(x, 0, RB), xdev(1))
    send(BX + 1, b_part(x, 0, RB), b_part(x, 0, RB), xdev(3))
    send(TOK + 2, tok_half(y, 0, T), tok_half(y, 0, T), twin)

    load_freq.wait()

    row = lax.broadcasted_iota(jnp.int32, (R, R), 0)
    col = lax.broadcasted_iota(jnp.int32, (R, R), 1)
    mirror = jnp.where(row + col == R - 1, 1.0, 0.0).astype(BF)
    unit = jnp.where(
        lax.broadcasted_iota(jnp.int32, (CB, CB), 0) == lax.broadcasted_iota(jnp.int32, (CB, CB), 1), 1.0, 0.0
    ).astype(BF)

    def odd_lanes(q):
        return (fbuf[:, pl.ds(pl.multiple_of(q * R, R), R)] & 1) == 1

    def build(q):
        counts = lax.broadcasted_iota(jnp.int32, (64, 128), 0)
        for h in range(2):
            f = fbuf[:, pl.ds(pl.multiple_of(q * R + h * 128, 128), 128)]
            scale = jnp.where(f == 0, math.sqrt(1.0 / D), math.sqrt(2.0 / D)).astype(F32)
            c, s = cos_sin((counts * 128 * f) & 32767)
            ca[...] = c * scale
            sa[...] = s * scale
            cb, sb = cos_sin(((2 * counts + 1) * f) & 32767)

            def step(a, carry):
                value = ca[pl.ds(a, 1)] * cb - sa[pl.ds(a, 1)] * sb
                table[q, pl.ds(pl.multiple_of(a * 64, 64), 64), pl.ds(h * 128, 128)] = value.astype(BF)
                return carry

            lax.fori_loop(0, 64, step, 0, unroll=4)

    def fold(j, carry):
        low = pl.ds(pl.multiple_of(j * R, R), R)
        high = pl.ds(pl.multiple_of(D - R - j * R, R), R)
        lows = 0.9 * state[low] + gbuf[low].astype(F32)
        highs = 0.9 * state[high] + gbuf[high].astype(F32)
        state[low] = lows
        state[high] = highs
        turned = dot(mirror, highs.astype(BF))
        xt[pl.ds(0, CB), low] = dot_nt(unit, (lows + turned).astype(BF)).astype(BF)
        xt[pl.ds(CB, CB), low] = dot_nt(unit, (lows - turned).astype(BF)).astype(BF)
        return carry

    def forward(q):
        both = dot(xt[...], table[q])
        odd = odd_lanes(q)
        own = jnp.where(odd, both[CB:], both[:CB]).astype(BF)
        coef[q] = own
        zero = jnp.zeros_like(own)
        seo[q, pl.ds(0, CB)] = jnp.where(odd, zero, own)
        seo[q, pl.ds(CB, CB)] = jnp.where(odd, own, zero)

    def inverse(j, carry):
        low = pl.ds(pl.multiple_of(j * R, R), R)
        high = pl.ds(pl.multiple_of(D - R - j * R, R), R)
        total = dot_nt(table[0, low], seo[0])
        for q in range(1, X):
            total += dot_nt(table[q, low], seo[q])
        even, odd = total[:, :CB], total[:, CB:]
        state[low] -= even + odd
        state[high] -= dot(mirror, (even - odd).astype(BF))
        pltpu.make_async_copy(state.at[low], res.at[0, low], stsem.at[2 * j]).start()
        pltpu.make_async_copy(state.at[high], res.at[0, high], stsem.at[2 * j + 1]).start()
        return carry

    def send_coef(d):
        send(CX + d - 1, coef.at[(x + d) % X], rsx.at[d - 1], xdev(d))

    build((x + 2) % X)
    for s in range(4):
        for a, b in loads[2 * s:2 * s + 2]:
            a.wait()
            b.wait()
        lax.fori_loop(4 * s, 4 * s + 4, fold, 0)
    a_right_in(0)
    a_right(1)
    a_left_in(0)
    a_left(1)
    arrived(BX + 0, b_part(x + 3, 0, RB))
    send(BX + 2, b_part(x + 3, 0, RB // 2), b_part(x + 3, 0, RB // 2), xdev(1))
    arrived(BX + 1, b_part(x + 1, 0, RB))
    send(BX + 3, b_part(x + 1, RB // 2, RB // 2), b_part(x + 1, RB // 2, RB // 2), xdev(3))
    forward((x + 2) % X)
    send_coef(2)
    build((x + 1) % X)
    a_right_in(1)
    a_right(2)
    a_left_in(1)
    a_left(2)
    arrived(BX + 2, b_part(x + 2, 0, RB // 2))
    arrived(BX + 3, b_part(x + 2, RB // 2, RB // 2))
    b_right(0)
    b_left(0)
    forward((x + 1) % X)
    send_coef(1)
    build((x + 3) % X)
    arrived(TOK + 0, tok_half(y + 3, 0, T))
    send(TOK + 3, tok_half(y + 3, 0, T // 2), tok_half(y + 3, 0, T // 2), ydev(1))
    send(TOK + 5, tok_half(y + 3, 0, T), tok_half(y + 3, 0, T), twin)
    arrived(TOK + 1, tok_half(y + 1, 0, T))
    send(TOK + 4, tok_half(y + 1, T // 2, T // 2), tok_half(y + 1, T // 2, T // 2), ydev(3))
    send(TOK + 6, tok_half(y + 1, 0, T), tok_half(y + 1, 0, T), twin)
    forward((x + 3) % X)
    send_coef(3)
    a_right_in(2)
    a_right(3)
    a_left_in(2)
    build(x)
    b_right_in(0)
    b_right(1)
    b_left_in(0)
    b_left(1)
    forward(x)

    total = coef[x].astype(F32)
    for d in range(1, X):
        arrived(CX + d - 1, rsx.at[d - 1])
    for d in range(1, X):
        total += rsx[d - 1].astype(F32)
    rszs[...] = total.astype(BF).reshape(Z, 16, R)
    for d in range(1, Z):
        send(CZ + d - 1, rszs.at[(z + d) % Z], rszr.at[d - 1], zdev(d))
    a_right_in(3)
    send(AX + 0, a_plane(x, 0, Z), a_plane(x, 0, Z), xdev(1))
    send(AX + 1, a_plane(x, 0, Z), a_plane(x, 0, Z), xdev(3))
    b_right_in(1)
    b_right(2)
    b_left_in(1)
    b_left(2)
    lax.fori_loop(0, 6, inverse, 0)
    for d in range(1, Z):
        arrived(CZ + d - 1, rszr.at[d - 1])
    part = rszs[z].astype(F32)
    for d in range(1, Z):
        part += rszr[d - 1].astype(F32)

    def s_rows(xx, zz):
        return sbuf.at[xx % X, pl.ds(pl.multiple_of((zz % Z) * 16, 16), 16)]

    sbuf[x, pl.ds(pl.multiple_of(z * 16, 16), 16)] = (part * (1.0 / REPLICAS)).astype(BF)
    for d in range(1, Z):
        send(GZ + d - 1, s_rows(x, z), s_rows(x, z), zdev(d))
    b_right_in(2)
    b_left_in(2)
    b_left(3)
    arrived(TOK + 3, tok_half(y + 2, 0, T // 2))
    arrived(TOK + 4, tok_half(y + 2, T // 2, T // 2))
    send(TOK + 7, tok_half(y + 2, 0, T), tok_half(y + 2, 0, T), twin)
    lax.fori_loop(6, 12, inverse, 0)
    for d in range(1, Z):
        arrived(GZ + d - 1, s_rows(x, z - d + Z))
    for d in range(1, X):
        send(GX + d - 1, sbuf.at[x], sbuf.at[x], xdev(d))
    lax.fori_loop(12, 16, inverse, 0)

    arrived(TOK + 2, tok_twin(y))
    arrived(TOK + 5, tok_twin(y + 3))
    arrived(TOK + 6, tok_twin(y + 1))
    arrived(TOK + 7, tok_twin(y + 2))
    for j in range(H // R):
        b, o = j // 4, j % 4
        lows = tok[b, :, o * R:(o + 1) * R].astype(F32)
        turned = dot(tok[7 - b, :, (3 - o) * R:(4 - o) * R], mirror)
        tt[0:T, j * R:(j + 1) * R] = (lows + turned).astype(BF)
        tt[T:2 * T, j * R:(j + 1) * R] = (lows - turned).astype(BF)
    second = i >= REPLICAS // 2
    place = jnp.where(second, REPLICAS - 1 - i, i)
    pick = jnp.where(col == jnp.where(second, R - 1 - row, row), 1.0, 0.0).astype(BF)

    def token_step(q, carry):
        both = dot(tt[...], table[q])
        odd = odd_lanes(q)
        left[q, pl.ds(R, T)] = jnp.where(odd, both[T:], both[:T]).astype(BF)
        own = dot(pick, table[q, pl.ds(pl.multiple_of(place * R, R), R)])
        left[q, pl.ds(0, R)] = jnp.where(jnp.logical_and(odd, second), -own, own).astype(BF)
        return carry

    lax.fori_loop(0, X, token_step, 0)

    arrived(AX + 0, a_plane(x + 3, 0, Z))
    send(AX + 2, a_plane(x + 3, 0, Z // 2), a_plane(x + 3, 0, Z // 2), xdev(1))
    arrived(AX + 1, a_plane(x + 1, 0, Z))
    send(AX + 3, a_plane(x + 1, Z // 2, Z // 2), a_plane(x + 1, Z // 2, Z // 2), xdev(3))
    b_left_in(3)

    product = dot_nt(left[x], sbuf[x])
    for d in range(1, X):
        arrived(GX + d - 1, sbuf.at[(x - d + X) % X])
        product += dot_nt(left[(x - d + X) % X], sbuf[(x - d + X) % X])
    newm[...] = mbuf[...] - product[:R]

    arrived(AX + 2, a_plane(x + 2, 0, Z // 2))
    arrived(AX + 3, a_plane(x + 2, Z // 2, Z // 2))
    found = -product[R:]
    for b in range(8):
        found += dot(tok[b], wbuf[b // 2, pl.ds((b % 2) * 4, 4)].reshape(1024, CB))
    keys[...] = (found * D ** -0.5).astype(BF)

    for copy in sent:
        copy.wait_send()

    def drain(j, carry):
        low = pl.ds(pl.multiple_of(j * R, R), R)
        high = pl.ds(pl.multiple_of(D - R - j * R, R), R)
        pltpu.make_async_copy(state.at[low], res.at[0, low], stsem.at[2 * j]).wait()
        pltpu.make_async_copy(state.at[high], res.at[0, high], stsem.at[2 * j + 1]).wait()
        return carry

    lax.fori_loop(0, H // R, drain, 0)


def body(momentum, gradient, masters, tokens, freq_index):
    hbm = pl.BlockSpec(memory_space=pl.ANY)
    vmem = pl.BlockSpec(memory_space=pltpu.VMEM)
    return pl.pallas_call(
        kernel,
        out_shape=(
            jax.ShapeDtypeStruct((1, D, CB), F32),
            jax.ShapeDtypeStruct((R, CB), F32),
            jax.ShapeDtypeStruct((T, CB), BF),
        ),
        in_specs=[hbm] * 5,
        out_specs=(hbm, vmem, vmem),
        scratch_shapes=[
            pltpu.VMEM((D, CB), F32),
            pltpu.VMEM((D, CB), BF),
            pltpu.VMEM((X, H, R), BF),
            pltpu.VMEM((2 * CB, H), BF),
            pltpu.VMEM((X, 2 * CB, R), BF),
            pltpu.VMEM((X, CB, R), BF),
            pltpu.VMEM((X - 1, CB, R), BF),
            pltpu.VMEM((Z, 16, R), BF),
            pltpu.VMEM((Z - 1, 16, R), BF),
            pltpu.VMEM((X, CB, R), BF),
            pltpu.VMEM((8, T, 1024), BF),
            pltpu.VMEM((2 * T, H), BF),
            pltpu.VMEM((X, R + T, R), BF),
            pltpu.VMEM((X, Z, R, CB), BF),
            pltpu.VMEM((R, CB), F32),
            pltpu.VMEM((1, K), jnp.int32),
            pltpu.VMEM((64, 128), F32),
            pltpu.VMEM((64, 128), F32),
            pltpu.SemaphoreType.DMA((19,)),
            pltpu.SemaphoreType.DMA((32,)),
            pltpu.SemaphoreType.DMA((MSGS,)),
            pltpu.SemaphoreType.DMA((MSGS,)),
        ],
        compiler_params=pltpu.CompilerParams(
            collective_id=0, has_side_effects=True, vmem_limit_bytes=56 * 1024 * 1024),
    )(momentum, gradient, masters, tokens, freq_index)


def solution(mesh):
    return jax.shard_map(
        body,
        mesh=mesh,
        in_specs=(
            P("dp", None, "tensor"),
            P("dp", None, "tensor"),
            P("dp", "tensor"),
            P("dp", "tensor"),
            P("tensor", None),
        ),
        out_specs=(P("dp", None, "tensor"), P("dp", "tensor"), P("dp", "tensor")),
        check_vma=False,
    )
```

time: 639 us -> 58.2 us (0.09)
  the two profiles are of different devices: /device:TPU:8 before, /device:TPU:24 now
where the time goes in v1:
time: 58.2 us; the launch traced here: 58.1 us
  Pallas kernels  51.6 us (89%)
  local copies, waits for them, and re-layouts  5.78 us (10%)
  between operations  0.66 us (1%)
    pallas_call x1, Pallas kernels, body(): pl.pallas_call(kernel, out_shape=(jax.ShapeDtypeStruct((1, D, CB), F32),...  51.6 us
    unnamed x7, local copies, waits for them, and re-layouts  5.78 us

profile of v1, /device:TPU:24, one launch (start us, length us, event | category | flops | bytes accessed | tf_op | source)
XLA Modules:
  0.0 58.1 jit_solution(16885156490518543652)
XLA Ops:
  0.6 51.6 %shard_map.76 = (f32[1,8192,128]{2,1,0:T(8,128)}, f32[256,128]{1,0:T(8,128)}, bf16[128,128]{1,0:T(8,128)(2,1)}) custom-call(f32[1,8192,128]{2,1,0:T(8,128)} %mom.1, bf16[1,8192,128]{2,1,0:T(8,128)(2,1)} %grad.1, f32[256,128]{1,0:T(8,128)} %mast.1, bf16[128,1024]{1,0:T(8,128)(2,1)} %tok_in.1, s32[1,1024]{1,0:T(1,128)} %freq.1), custom_call_target="tpu_custom_call" | custom-call | tf_op jit(solution)/shard_map/pallas_call | solution.py:368
  52.3 0.0 copy-start
  52.3 0.0 copy-start.1
  52.3 4.5 %copy.11 = f32[1,8192,128]{2,1,0:T(8,128)} copy(f32[1,8192,128]{2,1,0:T(8,128)} %get-tuple-element.6) | data formatting | bytes 8388608
  56.8 0.0 copy-done
  56.8 0.7 %copy.12 = f32[256,128]{1,0:T(8,128)} copy(f32[256,128]{1,0:T(8,128)S(1)} %copy-done) | data formatting | bytes 262144
  57.5 0.0 copy-done.1
  57.5 0.6 %copy.13 = bf16[128,128]{1,0:T(8,128)(2,1)} copy(bf16[128,128]{1,0:T(8,128)(2,1)S(1)} %copy-done.1) | data formatting | bytes 65536
Async XLA Ops:
  52.3 4.5 %copy-start = (f32[256,128]{1,0:T(8,128)S(1)}, f32[256,128]{1,0:T(8,128)}, u32[]{:S(2)}) copy-start(f32[256,128]{1,0:T(8,128)} %get-tuple-element.7) | copy-start | bytes 393220
  52.3 5.2 %copy-start.1 = (bf16[128,128]{1,0:T(8,128)(2,1)S(1)}, bf16[128,128]{1,0:T(8,128)(2,1)}, u32[]{:S(2)}) copy-start(bf16[128,128]{1,0:T(8,128)(2,1)} %get-tuple-element.8) | copy-start | bytes 98308

commit v2 on v1

v2 whole, which is shorter than its diff:
```python
import math

import jax
import jax.numpy as jnp
from jax import lax
from jax.experimental import pallas as pl
from jax.experimental.pallas import tpu as pltpu
from jax.sharding import PartitionSpec as P

D = 8192
H = D // 2
K = 1024
CB = 128
X, Z = 4, 8
REPLICAS = X * Z
R = 256
T = 128
BF = jnp.bfloat16
F32 = jnp.float32

TOK, MZ, XP, XM, FP, FM, CX, CZ, GZ, GX, MSGS = 0, 8, 15, 23, 31, 35, 39, 42, 49, 56, 59
PASS_P, PASS_M = (0, 1, 2, 3), (7, 6, 5, 4)


def dot(a, b):
    return jnp.dot(a, b, preferred_element_type=F32)


def dot_nt(a, b):
    return lax.dot_general(a, b, (((1,), (1,)), ((), ())), preferred_element_type=F32)


def cos_sin(phase):
    quadrant = (phase + 4096) >> 13
    angle = (phase - (quadrant << 13)).astype(F32) * (math.pi / 16384)
    square = angle * angle
    sine = angle * (1.0 + square * (-1 / 6 + square * (1 / 120 + square * (-1 / 5040))))
    cosine = 1.0 + square * (-0.5 + square * (1 / 24 + square * (-1 / 720 + square * (1 / 40320))))
    swap = (quadrant & 1) == 1
    c = jnp.where(swap, sine, cosine)
    s = jnp.where(swap, cosine, sine)
    c = jnp.where(((quadrant + 1) & 2) == 2, -c, c)
    s = jnp.where((quadrant & 2) == 2, -s, s)
    return c, s


def kernel(mom, grad, mast, tok_in, freq, res, newm, keys,
           gbuf, table, xt, seo, coef, rsx, rszs, rszr, sbuf, tok, tt, left, wbuf, mbuf, fbuf, frel, acc,
           ca, sa, ldsem, ssem, rsem):
    i = lax.axis_index("dp")
    t = lax.axis_index("tensor")
    x, z = i // Z, i % Z
    y, core = t // 2, t % 2

    def xdev(d):
        return (((x + d) % X) * Z + z, t)

    def zdev(d):
        return (x * Z + (z + d) % Z, t)

    def ydev(d):
        return (i, ((y + d) % 4) * 2 + core)

    twin = (i, y * 2 + (1 - core))

    barrier = pltpu.get_barrier_semaphore()
    peers = [xdev(d) for d in range(1, X)] + [zdev(d) for d in range(1, Z)] + [ydev(1), ydev(3), twin]
    for peer in peers:
        pl.semaphore_signal(barrier, inc=1, device_id=peer, device_id_type=pl.DeviceIdType.MESH)

    load_mast = pltpu.make_async_copy(mast, mbuf, ldsem.at[0])
    load_freq = pltpu.make_async_copy(freq, fbuf, ldsem.at[1])
    load_tok = pltpu.make_async_copy(tok_in, tok.at[t], ldsem.at[2])
    load_mast.start()
    load_tok.start()
    load_freq.start()
    loads = []
    for c in (0, 7, 1, 6, 2, 5, 3, 4):
        rows = pl.ds(1024 * c, 1024)
        a = pltpu.make_async_copy(mom.at[0, rows], res.at[0, rows], ldsem.at[3 + c])
        b = pltpu.make_async_copy(grad.at[0, rows], gbuf.at[rows], ldsem.at[11 + c])
        a.start()
        b.start()
        loads.append((a, b))

    sent = []

    def send(number, src, dst, device):
        copy = pltpu.make_async_remote_copy(
            src_ref=src, dst_ref=dst, send_sem=ssem.at[number], recv_sem=rsem.at[number],
            device_id=device, device_id_type=pl.DeviceIdType.MESH)
        copy.start()
        sent.append(copy)

    def arrived(number, ref):
        pltpu.make_async_remote_copy(
            src_ref=ref, dst_ref=ref, send_sem=ssem.at[number], recv_sem=rsem.at[number],
            device_id=twin, device_id_type=pl.DeviceIdType.MESH).wait_recv()

    load_mast.wait()
    wbuf[x, z] = mbuf[...].astype(BF)
    load_tok.wait()
    pl.semaphore_wait(barrier, len(peers))

    def block(dx, dz):
        return wbuf.at[(x + dx) % X, (z + dz) % Z]

    def spread(dz):
        send(XP + dz, block(0, dz), block(0, dz), xdev(1))
        send(XM + dz, block(0, dz), block(0, dz), xdev(3))

    def from_z(*offsets):
        for dz in offsets:
            arrived(MZ + (Z - dz) - 1, block(0, dz))
            spread(dz)

    def from_x(*offsets):
        for dz in offsets:
            arrived(XP + dz, block(3, dz))
            if dz in PASS_P:
                send(FP + PASS_P.index(dz), block(3, dz), block(3, dz), xdev(1))
            arrived(XM + dz, block(1, dz))
            if dz in PASS_M:
                send(FM + PASS_M.index(dz), block(1, dz), block(1, dz), xdev(3))

    def tok_half(yy, lo, n):
        return tok.at[(yy % 4) * 2 + core, pl.ds(lo, n)]

    def tok_twin(yy):
        return tok.at[(yy % 4) * 2 + 1 - core]

    send(TOK + 0, tok_half(y, 0, T), tok_half(y, 0, T), ydev(1))
    send(TOK + 1, tok_half(y, 0, T), tok_half(y, 0, T), ydev(3))
    for d in (1, 7, 2, 6, 3, 5, 4):
        send(MZ + d - 1, block(0, 0), block(0, 0), zdev(d))
    spread(0)
    send(TOK + 2, tok_half(y, 0, T), tok_half(y, 0, T), twin)

    load_freq.wait()
    for d in range(X):
        frel[:, d * R:(d + 1) * R] = fbuf[:, pl.ds(pl.multiple_of(((x + d) % X) * R, R), R)]

    row = lax.broadcasted_iota(jnp.int32, (R, R), 0)
    col = lax.broadcasted_iota(jnp.int32, (R, R), 1)
    mirror = jnp.where(row + col == R - 1, 1.0, 0.0).astype(BF)
    unit = jnp.where(
        lax.broadcasted_iota(jnp.int32, (CB, CB), 0) == lax.broadcasted_iota(jnp.int32, (CB, CB), 1), 1.0, 0.0
    ).astype(BF)

    def angles(d):
        counts = lax.broadcasted_iota(jnp.int32, (64, 128), 0)
        waves = []
        for h in range(2):
            f = frel[:, d * R + h * 128:d * R + (h + 1) * 128]
            scale = jnp.where(f == 0, math.sqrt(1.0 / D), math.sqrt(2.0 / D)).astype(F32)
            c, s = cos_sin((counts * 128 * f) & 32767)
            ca[h] = c * scale
            sa[h] = s * scale
            waves.append(cos_sin(((2 * counts + 1) * f) & 32767))
        return waves

    def build(d, b, waves):
        base = pl.multiple_of(b * 1024, 1024)
        for n in range(16):
            for h in range(2):
                cb, sb = waves[h]
                value = ca[h, pl.ds(b * 16 + n, 1)] * cb - sa[h, pl.ds(b * 16 + n, 1)] * sb
                table[pl.ds(base + n * 64, 64), d * R + h * 128:d * R + (h + 1) * 128] = value.astype(BF)

    def fold(j):
        low = slice(j * R, (j + 1) * R)
        high = slice(D - (j + 1) * R, D - j * R)
        lows = 0.9 * res[0, low] + gbuf[low].astype(F32)
        highs = 0.9 * res[0, high] + gbuf[high].astype(F32)
        res[0, low] = lows
        res[0, high] = highs
        turned = dot(mirror, highs.astype(BF))
        xt[0:CB, low] = dot_nt(unit, (lows + turned).astype(BF)).astype(BF)
        xt[CB:2 * CB, low] = dot_nt(unit, (lows - turned).astype(BF)).astype(BF)

    def split(d, both):
        lanes = slice(d * R, (d + 1) * R)
        odd = (frel[:, lanes] & 1) == 1
        own = jnp.where(odd, both[CB:], both[:CB]).astype(BF)
        coef[d] = own
        zero = jnp.zeros_like(own)
        seo[0:CB, lanes] = jnp.where(odd, zero, own)
        seo[CB:2 * CB, lanes] = jnp.where(odd, own, zero)

    def build_forward(d):
        waves = angles(d)
        acc[...] = jnp.zeros_like(acc)

        def step(b, carry):
            build(d, b, waves)
            rows = pl.ds(pl.multiple_of(b * 1024, 1024), 1024)
            acc[...] += dot(xt[:, rows], table[rows, d * R:(d + 1) * R])
            return carry

        lax.fori_loop(0, 4, step, 0)
        split(d, acc[...])

    M = 512

    def inverse(j, carry):
        total = dot_nt(table[pl.ds(pl.multiple_of(j * M, M), M)], seo[...])
        for n in range(M // R):
            low = pl.ds(pl.multiple_of(j * M, M) + n * R, R)
            high = pl.ds(pl.multiple_of(D - M - j * M, M) + (M - R - n * R), R)
            even, odd = total[n * R:(n + 1) * R, :CB], total[n * R:(n + 1) * R, CB:]
            res[0, low] -= even + odd
            res[0, high] -= dot(mirror, (even - odd).astype(BF))
        return carry

    def send_coef(d):
        send(CX + d - 1, coef.at[d], rsx.at[d - 1], xdev(d))

    waves = angles(2)

    def first(b, carry):
        build(2, b, waves)
        return carry

    lax.fori_loop(0, 4, first, 0)
    for s in range(4):
        for a, b in loads[2 * s:2 * s + 2]:
            a.wait()
            b.wait()
        for j in range(4 * s, 4 * s + 4):
            fold(j)
    split(2, dot(xt[...], table[:, 2 * R:3 * R]))
    send_coef(2)
    from_z(1, 7)
    build_forward(1)
    send_coef(1)
    arrived(TOK + 0, tok_half(y + 3, 0, T))
    send(TOK + 3, tok_half(y + 3, 0, T // 2), tok_half(y + 3, 0, T // 2), ydev(1))
    send(TOK + 5, tok_half(y + 3, 0, T), tok_half(y + 3, 0, T), twin)
    arrived(TOK + 1, tok_half(y + 1, 0, T))
    send(TOK + 4, tok_half(y + 1, T // 2, T // 2), tok_half(y + 1, T // 2, T // 2), ydev(3))
    send(TOK + 6, tok_half(y + 1, 0, T), tok_half(y + 1, 0, T), twin)
    build_forward(3)
    send_coef(3)
    from_z(2, 6)
    from_x(0)
    build_forward(0)

    total = coef[0].astype(F32)
    for d in range(1, X):
        arrived(CX + d - 1, rsx.at[d - 1])
        total += rsx[d - 1].astype(F32)
    rszs[...] = total.astype(BF).reshape(Z, 16, R)
    for d in (4, 3, 5, 2, 6, 1, 7):
        send(CZ + d - 1, rszs.at[(z + d) % Z], rszr.at[d - 1], zdev(d))
    from_z(3, 5, 4)
    from_x(1, 7)
    lax.fori_loop(0, 4, inverse, 0)
    part = rszs[z].astype(F32)
    for d in range(1, Z):
        arrived(CZ + d - 1, rszr.at[d - 1])
        part += rszr[d - 1].astype(F32)

    def s_rows(zz):
        return sbuf.at[0, pl.ds(pl.multiple_of((zz % Z) * 16, 16), 16)]

    sbuf[0, pl.ds(pl.multiple_of(z * 16, 16), 16)] = (part * (1.0 / REPLICAS)).astype(BF)
    for d in (4, 3, 5, 2, 6, 1, 7):
        send(GZ + d - 1, s_rows(z), s_rows(z), zdev(d))
    from_x(2, 6)
    arrived(TOK + 3, tok_half(y + 2, 0, T // 2))
    arrived(TOK + 4, tok_half(y + 2, T // 2, T // 2))
    send(TOK + 7, tok_half(y + 2, 0, T), tok_half(y + 2, 0, T), twin)
    lax.fori_loop(4, 8, inverse, 0)
    for d in range(1, Z):
        arrived(GZ + d - 1, s_rows(z - d + Z))
    for d in (2, 1, 3):
        send(GX + d - 1, sbuf.at[0], sbuf.at[X - d], xdev(d))
    from_x(3, 5, 4)

    arrived(TOK + 2, tok_twin(y))
    arrived(TOK + 5, tok_twin(y + 3))
    arrived(TOK + 6, tok_twin(y + 1))
    arrived(TOK + 7, tok_twin(y + 2))
    for j in range(H // R):
        b, o = j // 4, j % 4
        lows = tok[b, :, o * R:(o + 1) * R].astype(F32)
        turned = dot(tok[7 - b, :, (3 - o) * R:(4 - o) * R], mirror)
        tt[0:T, j * R:(j + 1) * R] = (lows + turned).astype(BF)
        tt[T:2 * T, j * R:(j + 1) * R] = (lows - turned).astype(BF)
    second = i >= REPLICAS // 2
    place = jnp.where(second, REPLICAS - 1 - i, i)
    pick = jnp.where(col == jnp.where(second, R - 1 - row, row), 1.0, 0.0).astype(BF)

    def token_step(d, carry):
        lanes = pl.ds(pl.multiple_of(d * R, R), R)
        both = dot(tt[...], table[:, lanes])
        odd = (frel[:, lanes] & 1) == 1
        left[pl.ds(R, T), lanes] = jnp.where(odd, both[T:], both[:T]).astype(BF)
        own = dot(pick, table[pl.ds(pl.multiple_of(place * R, R), R), lanes])
        left[pl.ds(0, R), lanes] = jnp.where(jnp.logical_and(odd, second), -own, own).astype(BF)
        return carry

    lax.fori_loop(0, X, token_step, 0)

    def plane(dx):
        xx = (x + dx) % X
        return (dot(tok[2 * xx], wbuf[xx, 0:4].reshape(1024, CB))
                + dot(tok[2 * xx + 1], wbuf[xx, 4:8].reshape(1024, CB)))

    found = plane(0) + plane(1) + plane(3)
    for n in range(4):
        arrived(FP + n, block(2, PASS_P[n]))
        arrived(FM + n, block(2, PASS_M[n]))
    found += plane(2)
    product = dot_nt(left[:, 0:R], sbuf[0])
    for d in range(1, X):
        arrived(GX + d - 1, sbuf.at[X - d])
        product += dot_nt(left[:, (X - d) * R:(X - d + 1) * R], sbuf[X - d])
    newm[...] = mbuf[...] - product[:R]
    keys[...] = ((found - product[R:]) * D ** -0.5).astype(BF)

    for copy in sent:
        copy.wait_send()


def store(res, newm, keys, res_out, newm_out, keys_out, sem):
    copies = [
        pltpu.make_async_copy(res, res_out, sem.at[0]),
        pltpu.make_async_copy(newm, newm_out, sem.at[1]),
        pltpu.make_async_copy(keys, keys_out, sem.at[2]),
    ]
    for copy in copies:
        copy.start()
    for copy in copies:
        copy.wait()


def body(momentum, gradient, masters, tokens, freq_index):
    hbm = pl.BlockSpec(memory_space=pl.ANY)
    vmem = pl.BlockSpec(memory_space=pltpu.VMEM)
    held = pl.pallas_call(
        kernel,
        out_shape=(
            pltpu.VMEM((1, D, CB), F32),
            pltpu.VMEM((R, CB), F32),
            pltpu.VMEM((T, CB), BF),
        ),
        in_specs=[hbm] * 5,
        out_specs=(vmem, vmem, vmem),
        scratch_shapes=[
            pltpu.VMEM((D, CB), BF),
            pltpu.VMEM((H, K), BF),
            pltpu.VMEM((2 * CB, H), BF),
            pltpu.VMEM((2 * CB, K), BF),
            pltpu.VMEM((X, CB, R), BF),
            pltpu.VMEM((X - 1, CB, R), BF),
            pltpu.VMEM((Z, 16, R), BF),
            pltpu.VMEM((Z - 1, 16, R), BF),
            pltpu.VMEM((X, CB, R), BF),
            pltpu.VMEM((8, T, 1024), BF),
            pltpu.VMEM((2 * T, H), BF),
            pltpu.VMEM((R + T, K), BF),
            pltpu.VMEM((X, Z, R, CB), BF),
            pltpu.VMEM((R, CB), F32),
            pltpu.VMEM((1, K), jnp.int32),
            pltpu.VMEM((1, K), jnp.int32),
            pltpu.VMEM((R, R), F32),
            pltpu.VMEM((2, 64, 128), F32),
            pltpu.VMEM((2, 64, 128), F32),
            pltpu.SemaphoreType.DMA((19,)),
            pltpu.SemaphoreType.DMA((MSGS,)),
            pltpu.SemaphoreType.DMA((MSGS,)),
        ],
        compiler_params=pltpu.CompilerParams(
            collective_id=0, has_side_effects=True, vmem_limit_bytes=56 * 1024 * 1024),
    )(momentum, gradient, masters, tokens, freq_index)
    return pl.pallas_call(
        store,
        out_shape=(
            jax.ShapeDtypeStruct((1, D, CB), F32),
            jax.ShapeDtypeStruct((R, CB), F32),
            jax.ShapeDtypeStruct((T, CB), BF),
        ),
        in_specs=[vmem] * 3,
        out_specs=(hbm, hbm, hbm),
        scratch_shapes=[pltpu.SemaphoreType.DMA((3,))],
        compiler_params=pltpu.CompilerParams(vmem_limit_bytes=4 * 1024 * 1024),
    )(*[pltpu.with_memory_space_constraint(a, pltpu.VMEM) for a in held])


def solution(mesh):
    return jax.shard_map(
        body,
        mesh=mesh,
        in_specs=(
            P("dp", None, "tensor"),
            P("dp", None, "tensor"),
            P("dp", "tensor"),
            P("dp", "tensor"),
            P("tensor", None),
        ),
        out_specs=(P("dp", None, "tensor"), P("dp", "tensor"), P("dp", "tensor")),
        check_vma=False,
    )
```

time: 58.2 us -> 42.6 us (0.73)
  the two profiles are of different devices: /device:TPU:24 before, /device:TPU:2 now
where the time goes in v2:
time: 42.6 us; the launch traced here: 42.5 us
  Pallas kernels  41.9 us (98%)
  between operations  0.64 us (2%)
    pallas_call x1, Pallas kernels, body(): pl.pallas_call(kernel, out_shape=(pltpu.VMEM((1, D, CB), F32), pltpu.VMEM...  39.8 us
    pallas_call x1, Pallas kernels, body(): pl.pallas_call(store, out_shape=(jax.ShapeDtypeStruct((1, D, CB), F32), j...  2.07 us

profile of v2, /device:TPU:2, one launch (start us, length us, event | category | flops | bytes accessed | tf_op | source)
XLA Modules:
  0.0 42.5 jit_solution(7883373168998477015)
XLA Ops:
  0.6 39.8 %shard_map.76 = (f32[1,8192,128]{2,1,0:T(8,128)S(1)}, f32[256,128]{1,0:T(8,128)S(1)}, bf16[128,128]{1,0:T(8,128)(2,1)S(1)}) custom-call(f32[1,8192,128]{2,1,0:T(8,128)} %mom.1, bf16[1,8192,128]{2,1,0:T(8,128)(2,1)} %grad.1, f32[256,128]{1,0:T(8,128)} %mast.1, bf16[128,1024]{1,0:T(8,128)(2,1)} %tok_in.1, s32[1,1024]{1,0:T(1,128)} %freq.1), custom_call_target="tpu_custom_call" | custom-call | tf_op jit(solution)/shard_map/pallas_call | solution.py:341
  40.4 2.1 %shard_map.77 = (f32[1,8192,128]{2,1,0:T(8,128)}, f32[256,128]{1,0:T(8,128)}, bf16[128,128]{1,0:T(8,128)(2,1)}) custom-call(f32[1,8192,128]{2,1,0:T(8,128)S(1)} %get-tuple-element.6.res, f32[256,128]{1,0:T(8,128)S(1)} %get-tuple-element.7.newm, bf16[128,128]{1,0:T(8,128)(2,1)S(1)} %get-tuple-element.8.keys), custom_call_target="tpu_custom_call" | custom-call | tf_op jit(solution)/shard_map/pallas_call | solution.py:377

commit v3 on v2

--- a/solution.py
+++ b/solution.py
@@ -131,7 +131,7 @@
 
     send(TOK + 0, tok_half(y, 0, T), tok_half(y, 0, T), ydev(1))
     send(TOK + 1, tok_half(y, 0, T), tok_half(y, 0, T), ydev(3))
-    for d in (1, 7, 2, 6, 3, 5, 4):
+    for d in (1, 7, 2, 6):
         send(MZ + d - 1, block(0, 0), block(0, 0), zdev(d))
     spread(0)
     send(TOK + 2, tok_half(y, 0, T), tok_half(y, 0, T), twin)
@@ -175,8 +175,8 @@
         res[0, low] = lows
         res[0, high] = highs
         turned = dot(mirror, highs.astype(BF))
-        xt[0:CB, low] = dot_nt(unit, (lows + turned).astype(BF)).astype(BF)
-        xt[CB:2 * CB, low] = dot_nt(unit, (lows - turned).astype(BF)).astype(BF)
+        xt[0:CB, low] = (lows + turned).astype(BF).T
+        xt[CB:2 * CB, low] = (lows - turned).astype(BF).T
 
     def split(d, both):
         lanes = slice(d * R, (d + 1) * R)
@@ -200,7 +200,7 @@
         lax.fori_loop(0, 4, step, 0)
         split(d, acc[...])
 
-    M = 512
+    M = 1024
 
     def inverse(j, carry):
         total = dot_nt(table[pl.ds(pl.multiple_of(j * M, M), M)], seo[...])
@@ -228,6 +228,9 @@
             b.wait()
         for j in range(4 * s, 4 * s + 4):
             fold(j)
+        if s == 1:
+            for d in (3, 5, 4):
+                send(MZ + d - 1, block(0, 0), block(0, 0), zdev(d))
     split(2, dot(xt[...], table[:, 2 * R:3 * R]))
     send_coef(2)
     from_z(1, 7)
@@ -242,7 +245,6 @@
     build_forward(3)
     send_coef(3)
     from_z(2, 6)
-    from_x(0)
     build_forward(0)
 
     total = coef[0].astype(F32)
@@ -253,8 +255,10 @@
     for d in (4, 3, 5, 2, 6, 1, 7):
         send(CZ + d - 1, rszs.at[(z + d) % Z], rszr.at[d - 1], zdev(d))
     from_z(3, 5, 4)
+    from_x(0)
+    lax.fori_loop(0, 1, inverse, 0)
     from_x(1, 7)
-    lax.fori_loop(0, 4, inverse, 0)
+    lax.fori_loop(1, 2, inverse, 0)
     part = rszs[z].astype(F32)
     for d in range(1, Z):
         arrived(CZ + d - 1, rszr.at[d - 1])
@@ -266,16 +270,17 @@
     sbuf[0, pl.ds(pl.multiple_of(z * 16, 16), 16)] = (part * (1.0 / REPLICAS)).astype(BF)
     for d in (4, 3, 5, 2, 6, 1, 7):
         send(GZ + d - 1, s_rows(z), s_rows(z), zdev(d))
-    from_x(2, 6)
     arrived(TOK + 3, tok_half(y + 2, 0, T // 2))
     arrived(TOK + 4, tok_half(y + 2, T // 2, T // 2))
     send(TOK + 7, tok_half(y + 2, 0, T), tok_half(y + 2, 0, T), twin)
-    lax.fori_loop(4, 8, inverse, 0)
+    lax.fori_loop(2, 3, inverse, 0)
+    from_x(2, 6)
+    from_x(3, 5, 4)
+    lax.fori_loop(3, 4, inverse, 0)
     for d in range(1, Z):
         arrived(GZ + d - 1, s_rows(z - d + Z))
     for d in (2, 1, 3):
         send(GX + d - 1, sbuf.at[0], sbuf.at[X - d], xdev(d))
-    from_x(3, 5, 4)
 
     arrived(TOK + 2, tok_twin(y))
     arrived(TOK + 5, tok_twin(y + 3))

time: 42.6 us -> 41.4 us (0.972)
  Pallas kernels: 41.9 us -> 40.7 us
    pallas_call x1, Pallas kernels: 39.8 us -> 38.6 us  [body(): pl.pallas_call(kernel, out_shape=(pltpu.VMEM((1, D, CB), F32), pltpu.VMEM...]
where the time goes in v3:
time: 41.4 us; the launch traced here: 41.3 us
  Pallas kernels  40.7 us (98%)
  between operations  0.64 us (2%)
    pallas_call x1, Pallas kernels, body(): pl.pallas_call(kernel, out_shape=(pltpu.VMEM((1, D, CB), F32), pltpu.VMEM...  38.6 us
    pallas_call x1, Pallas kernels, body(): pl.pallas_call(store, out_shape=(jax.ShapeDtypeStruct((1, D, CB), F32), j...  2.07 us

profile of v3, /device:TPU:2, one launch (start us, length us, event | category | flops | bytes accessed | tf_op | source)
XLA Modules:
  0.0 41.3 jit_solution(8524849124506007853)
XLA Ops:
  0.6 38.6 %shard_map.76 = (f32[1,8192,128]{2,1,0:T(8,128)S(1)}, f32[256,128]{1,0:T(8,128)S(1)}, bf16[128,128]{1,0:T(8,128)(2,1)S(1)}) custom-call(f32[1,8192,128]{2,1,0:T(8,128)} %mom.1, bf16[1,8192,128]{2,1,0:T(8,128)(2,1)} %grad.1, f32[256,128]{1,0:T(8,128)} %mast.1, bf16[128,1024]{1,0:T(8,128)(2,1)} %tok_in.1, s32[1,1024]{1,0:T(1,128)} %freq.1), custom_call_target="tpu_custom_call" | custom-call | tf_op jit(solution)/shard_map/pallas_call | solution.py:346
  39.2 2.1 %shard_map.77 = (f32[1,8192,128]{2,1,0:T(8,128)}, f32[256,128]{1,0:T(8,128)}, bf16[128,128]{1,0:T(8,128)(2,1)}) custom-call(f32[1,8192,128]{2,1,0:T(8,128)S(1)} %get-tuple-element.6.res, f32[256,128]{1,0:T(8,128)S(1)} %get-tuple-element.7.newm, bf16[128,128]{1,0:T(8,128)(2,1)S(1)} %get-tuple-element.8.keys), custom_call_target="tpu_custom_call" | custom-call | tf_op jit(solution)/shard_map/pallas_call | solution.py:382

commit v4 on v3

--- a/solution.py
+++ b/solution.py
@@ -112,6 +112,11 @@
     def from_z(*offsets):
         for dz in offsets:
             arrived(MZ + (Z - dz) - 1, block(0, dz))
+            if dz == 6:
+                send(MZ + 2, block(0, 6), block(0, 6), zdev(1))
+                send(MZ + 3, block(0, 6), block(0, 6), zdev(2))
+            if dz == 2:
+                send(MZ + 4, block(0, 2), block(0, 2), zdev(Z - 1))
             spread(dz)
 
     def from_x(*offsets):
@@ -228,9 +233,6 @@
             b.wait()
         for j in range(4 * s, 4 * s + 4):
             fold(j)
-        if s == 1:
-            for d in (3, 5, 4):
-                send(MZ + d - 1, block(0, 0), block(0, 0), zdev(d))
     split(2, dot(xt[...], table[:, 2 * R:3 * R]))
     send_coef(2)
     from_z(1, 7)
@@ -242,9 +244,10 @@
     arrived(TOK + 1, tok_half(y + 1, 0, T))
     send(TOK + 4, tok_half(y + 1, T // 2, T // 2), tok_half(y + 1, T // 2, T // 2), ydev(3))
     send(TOK + 6, tok_half(y + 1, 0, T), tok_half(y + 1, 0, T), twin)
+    from_z(2, 6)
     build_forward(3)
     send_coef(3)
-    from_z(2, 6)
+    from_x(0)
     build_forward(0)
 
     total = coef[0].astype(F32)
@@ -255,7 +258,6 @@
     for d in (4, 3, 5, 2, 6, 1, 7):
         send(CZ + d - 1, rszs.at[(z + d) % Z], rszr.at[d - 1], zdev(d))
     from_z(3, 5, 4)
-    from_x(0)
     lax.fori_loop(0, 1, inverse, 0)
     from_x(1, 7)
     lax.fori_loop(1, 2, inverse, 0)

time: 41.4 us -> 40.9 us (0.988)
  Pallas kernels: 40.7 us -> 40.2 us
    pallas_call x1, Pallas kernels: 38.6 us -> 38.1 us  [body(): pl.pallas_call(kernel, out_shape=(pltpu.VMEM((1, D, CB), F32), pltpu.VMEM...]
where the time goes in v4:
time: 40.9 us
  Pallas kernels  40.2 us (98%)
  between operations  0.64 us (2%)
    pallas_call x1, Pallas kernels, body(): pl.pallas_call(kernel, out_shape=(pltpu.VMEM((1, D, CB), F32), pltpu.VMEM...  38.1 us
    pallas_call x1, Pallas kernels, body(): pl.pallas_call(store, out_shape=(jax.ShapeDtypeStruct((1, D, CB), F32), j...  2.07 us

profile of v4, /device:TPU:2, one launch (start us, length us, event | category | flops | bytes accessed | tf_op | source)
XLA Modules:
  0.0 40.9 jit_solution(6380550062442612638)
XLA Ops:
  0.6 38.1 %shard_map.76 = (f32[1,8192,128]{2,1,0:T(8,128)S(1)}, f32[256,128]{1,0:T(8,128)S(1)}, bf16[128,128]{1,0:T(8,128)(2,1)S(1)}) custom-call(f32[1,8192,128]{2,1,0:T(8,128)} %mom.1, bf16[1,8192,128]{2,1,0:T(8,128)(2,1)} %grad.1, f32[256,128]{1,0:T(8,128)} %mast.1, bf16[128,1024]{1,0:T(8,128)(2,1)} %tok_in.1, s32[1,1024]{1,0:T(1,128)} %freq.1), custom_call_target="tpu_custom_call" | custom-call | tf_op jit(solution)/shard_map/pallas_call | solution.py:348
  38.8 2.1 %shard_map.77 = (f32[1,8192,128]{2,1,0:T(8,128)}, f32[256,128]{1,0:T(8,128)}, bf16[128,128]{1,0:T(8,128)(2,1)}) custom-call(f32[1,8192,128]{2,1,0:T(8,128)S(1)} %get-tuple-element.6.res, f32[256,128]{1,0:T(8,128)S(1)} %get-tuple-element.7.newm, bf16[128,128]{1,0:T(8,128)(2,1)S(1)} %get-tuple-element.8.keys), custom_call_target="tpu_custom_call" | custom-call | tf_op jit(solution)/shard_map/pallas_call | solution.py:384

commit v5 on v4

--- a/solution.py
+++ b/solution.py
@@ -277,12 +277,12 @@
     send(TOK + 7, tok_half(y + 2, 0, T), tok_half(y + 2, 0, T), twin)
     lax.fori_loop(2, 3, inverse, 0)
     from_x(2, 6)
-    from_x(3, 5, 4)
     lax.fori_loop(3, 4, inverse, 0)
     for d in range(1, Z):
         arrived(GZ + d - 1, s_rows(z - d + Z))
     for d in (2, 1, 3):
         send(GX + d - 1, sbuf.at[0], sbuf.at[X - d], xdev(d))
+    from_x(3, 5, 4)
 
     arrived(TOK + 2, tok_twin(y))
     arrived(TOK + 5, tok_twin(y + 3))

time: 40.9 us -> 42.2 us (1.032)
  Pallas kernels: 40.2 us -> 41.5 us
    pallas_call x1, Pallas kernels: 38.1 us -> 39.4 us  [body(): pl.pallas_call(kernel, out_shape=(pltpu.VMEM((1, D, CB), F32), pltpu.VMEM...]
where the time goes in v5:
time: 42.2 us; the launch traced here: 42.1 us
  Pallas kernels  41.5 us (98%)
  between operations  0.64 us (2%)
    pallas_call x1, Pallas kernels, body(): pl.pallas_call(kernel, out_shape=(pltpu.VMEM((1, D, CB), F32), pltpu.VMEM...  39.4 us
    pallas_call x1, Pallas kernels, body(): pl.pallas_call(store, out_shape=(jax.ShapeDtypeStruct((1, D, CB), F32), j...  2.07 us

profile of v5, /device:TPU:2, one launch (start us, length us, event | category | flops | bytes accessed | tf_op | source)
XLA Modules:
  0.0 42.1 jit_solution(14301337489199149852)
XLA Ops:
  0.6 39.4 %shard_map.76 = (f32[1,8192,128]{2,1,0:T(8,128)S(1)}, f32[256,128]{1,0:T(8,128)S(1)}, bf16[128,128]{1,0:T(8,128)(2,1)S(1)}) custom-call(f32[1,8192,128]{2,1,0:T(8,128)} %mom.1, bf16[1,8192,128]{2,1,0:T(8,128)(2,1)} %grad.1, f32[256,128]{1,0:T(8,128)} %mast.1, bf16[128,1024]{1,0:T(8,128)(2,1)} %tok_in.1, s32[1,1024]{1,0:T(1,128)} %freq.1), custom_call_target="tpu_custom_call" | custom-call | tf_op jit(solution)/shard_map/pallas_call | solution.py:348
  40.1 2.1 %shard_map.77 = (f32[1,8192,128]{2,1,0:T(8,128)}, f32[256,128]{1,0:T(8,128)}, bf16[128,128]{1,0:T(8,128)(2,1)}) custom-call(f32[1,8192,128]{2,1,0:T(8,128)S(1)} %get-tuple-element.6.res, f32[256,128]{1,0:T(8,128)S(1)} %get-tuple-element.7.newm, bf16[128,128]{1,0:T(8,128)(2,1)S(1)} %get-tuple-element.8.keys), custom_call_target="tpu_custom_call" | custom-call | tf_op jit(solution)/shard_map/pallas_call | solution.py:384
